TPU v7x, 32 devices: a whole 2x2x4 slice. The times are simulated.
32 devices in a mesh: dp: 4 (over y, core), fsdp: 8 (over z, x).
Axes of the slice: x: 2, y: 2, z: 4, core: 2. Of those that a mesh axis runs over, the one named last changes fastest.
Arguments:
- stem_features: bfloat16 [32, 576, 1024], P(('dp', 'fsdp')), may hold values from -6 to 6
- lengths: int32 [32, 6], P(('dp', 'fsdp')), may hold values from 1 to 196, 576 in all within a row
- embed_weight: bfloat16 [1024, 768], P('fsdp'), may hold values from -0.1875 to 0.1875
- embed_bias: bfloat16 [768], P('fsdp'), may hold values from -1.5 to 1.5
- before_gain: bfloat16 [768], P('fsdp'), may hold values from 0.5 to 1.5
- before_shift: bfloat16 [768], P('fsdp'), may hold values from -1 to 1
- joint_weight: bfloat16 [768, 2304], P('fsdp'), may hold values from -0.21875 to 0.21875
- query_bias: bfloat16 [768], P('fsdp'), may hold values from -1.5 to 1.5
- value_bias: bfloat16 [768], P('fsdp'), may hold values from -1.5 to 1.5
- output_weight: bfloat16 [768, 768], P('fsdp'), may hold values from -1.75 to 1.75
- output_bias: bfloat16 [768], P('fsdp'), may hold values from -1.5 to 1.5
- middle_gain: bfloat16 [768], P('fsdp'), may hold values from 0.5 to 1.5
- middle_shift: bfloat16 [768], P('fsdp'), may hold values from -1 to 1
- expand_weight: bfloat16 [768, 3072], P('fsdp'), may hold values from -0.21875 to 0.21875
- expand_bias: bfloat16 [3072], P('fsdp'), may hold values from -1.5 to 1.5
- shrink_weight: bfloat16 [3072, 768], P('fsdp'), may hold values from -0.109375 to 0.109375
- shrink_bias: bfloat16 [768], P('fsdp'), may hold values from -1.5 to 1.5
- cotangent: bfloat16 [32, 576, 768], P(('dp', 'fsdp')), may hold values from -6 to 6
Outputs:
- activations: bfloat16 [32, 576, 768], P(('dp', 'fsdp'))
- stem_gradient: bfloat16 [32, 576, 1024], P(('dp', 'fsdp'))
- embed_weight_gradient: float32 [1024, 768], P('fsdp')
- embed_bias_gradient: float32 [768], P('fsdp')
- before_gain_gradient: float32 [768], P('fsdp')
- before_shift_gradient: float32 [768], P('fsdp')
- joint_weight_gradient: float32 [768, 2304], P('fsdp')
- query_bias_gradient: float32 [768], P('fsdp')
- value_bias_gradient: float32 [768], P('fsdp')
- output_weight_gradient: float32 [768, 768], P('fsdp')
- output_bias_gradient: float32 [768], P('fsdp')
- middle_gain_gradient: float32 [768], P('fsdp')
- middle_shift_gradient: float32 [768], P('fsdp')
- expand_weight_gradient: float32 [768, 3072], P('fsdp')
- expand_bias_gradient: float32 [3072], P('fsdp')
- shrink_weight_gradient: float32 [3072, 768], P('fsdp')
- shrink_bias_gradient: float32 [768], P('fsdp')
Inputs may be any that keep to these rules, and one draw needn't show every extreme that they name: In each row the 6 region lengths sum to 576, and the largest of them is 196.
All inputs are finite; a program needn't handle non-finite values.
Results may differ from a plain program's by a relative error of at most 0.015.
Values may be sent and summed in bfloat16 or wider, within the bound.
A program may use at most 256 MiB of HBM per device.

v0:
```python
import math

import jax
import jax.numpy as jnp
from jax import lax
from jax.sharding import PartitionSpec as P

HEADS = 12
HEAD_DIM = 64


def normalize(values):
    center = values - jnp.mean(values, axis=-1, keepdims=True)
    scaled = lax.rsqrt(jnp.mean(center * center, axis=-1, keepdims=True) + 1e-06)
    return (center * scaled, scaled)


def norm_backward(upstream, unit, scaled, gain):
    gain_part = jnp.sum(upstream * unit, axis=0)
    shift_part = jnp.sum(upstream, axis=0)
    inner = upstream * gain
    result = scaled * (
        inner
        - jnp.mean(inner, axis=-1, keepdims=True)
        - unit * jnp.mean(inner * unit, axis=-1, keepdims=True)
    )
    return (result, gain_part, shift_part)


def region_mask(lengths, row_len):
    bounds = jnp.cumsum(lengths, axis=1)
    places = jnp.arange(row_len, dtype=jnp.int32)
    labels = jnp.sum((places[None, :, None] >= bounds[:, None, :]).astype(jnp.int32), axis=2)
    return labels[:, :, None] == labels[:, None, :]


def column_sum(matrix):
    return jnp.sum(matrix.astype(jnp.float32), axis=0)


def local(
    stem_features,
    lengths,
    embed_weight,
    embed_bias,
    before_gain,
    before_shift,
    joint_weight,
    query_bias,
    value_bias,
    output_weight,
    output_bias,
    middle_gain,
    middle_shift,
    expand_weight,
    expand_bias,
    shrink_weight,
    shrink_bias,
    cotangent,
):
    wide = jnp.float32
    narrow = jnp.bfloat16
    shards = (
        embed_weight,
        embed_bias,
        before_gain,
        before_shift,
        joint_weight,
        query_bias,
        value_bias,
        output_weight,
        output_bias,
        middle_gain,
        middle_shift,
        expand_weight,
        expand_bias,
        shrink_weight,
        shrink_bias,
    )
    gathered = (
        lax.all_gather(shards[0], "fsdp", axis=0, tiled=True),
        lax.all_gather(shards[1], "fsdp", axis=0, tiled=True),
        lax.all_gather(shards[2], "fsdp", axis=0, tiled=True),
        lax.all_gather(shards[3], "fsdp", axis=0, tiled=True),
        lax.all_gather(shards[4], "fsdp", axis=0, tiled=True),
        lax.all_gather(shards[5], "fsdp", axis=0, tiled=True),
        lax.all_gather(shards[6], "fsdp", axis=0, tiled=True),
        lax.all_gather(shards[7], "fsdp", axis=0, tiled=True),
        lax.all_gather(shards[8], "fsdp", axis=0, tiled=True),
        lax.all_gather(shards[9], "fsdp", axis=0, tiled=True),
        lax.all_gather(shards[10], "fsdp", axis=0, tiled=True),
        lax.all_gather(shards[11], "fsdp", axis=0, tiled=True),
        lax.all_gather(shards[12], "fsdp", axis=0, tiled=True),
        lax.all_gather(shards[13], "fsdp", axis=0, tiled=True),
        lax.all_gather(shards[14], "fsdp", axis=0, tiled=True),
    )
    (
        embedding,
        embed_offset,
        first_gain,
        first_shift,
        joint,
        query_offset,
        value_offset,
        outward,
        out_offset,
        second_gain,
        second_shift,
        expand,
        expand_offset,
        shrink,
        shrink_offset,
    ) = gathered
    rows, row_len, stem_width = stem_features.shape
    width = embed_weight.shape[1]
    tokens = rows * row_len
    factor = 1.0 / math.sqrt(HEAD_DIM)
    heads_shape = (rows, row_len, HEADS, HEAD_DIM)
    same_region = region_mask(lengths, row_len)[:, None]
    inputs = stem_features.reshape(tokens, stem_width)
    embedded = jnp.dot(inputs, embedding, preferred_element_type=wide) + embed_offset.astype(wide)
    unit_first, scale_first = normalize(embedded)
    normed = (unit_first * first_gain.astype(wide) + first_shift.astype(wide)).astype(narrow)
    joint_offset = jnp.concatenate(
        [query_offset, jnp.zeros_like(query_offset), value_offset]
    ).astype(wide)
    projected = (jnp.dot(normed, joint, preferred_element_type=wide) + joint_offset).astype(narrow)
    query = projected[:, :width].reshape(heads_shape)
    keys = projected[:, width : 2 * width].reshape(heads_shape)
    values = projected[:, 2 * width :].reshape(heads_shape)

    def masked_scores():
        products = jnp.einsum("rqhe,rkhe->rhqk", query, keys, preferred_element_type=wide) * factor
        return jnp.where(same_region, products, -1e30)

    scores = masked_scores()
    largest = jnp.max(scores, axis=-1, keepdims=True)
    expos = jnp.exp(scores - largest)
    totals = jnp.sum(expos, axis=-1, keepdims=True)
    log_total = largest + jnp.log(totals)
    attend = (expos / totals).astype(narrow)
    mixed = jnp.einsum("rhqk,rkhe->rqhe", attend, values, preferred_element_type=wide)
    mixed = mixed.reshape(tokens, width).astype(narrow)
    residual = (
        embedded + jnp.dot(mixed, outward, preferred_element_type=wide) + out_offset.astype(wide)
    )
    unit_second, scale_second = normalize(residual)
    normed_mid = (unit_second * second_gain.astype(wide) + second_shift.astype(wide)).astype(narrow)
    upper = jnp.dot(normed_mid, expand, preferred_element_type=wide) + expand_offset.astype(wide)
    hidden_wide, gelu_pull = jax.vjp(lambda inner: jax.nn.gelu(inner, approximate=False), upper)
    hidden = hidden_wide.astype(narrow)
    output = (
        residual + jnp.dot(hidden, shrink, preferred_element_type=wide) + shrink_offset.astype(wide)
    )
    activations = output.astype(narrow).reshape(rows, row_len, width)
    backward_set = (
        lax.all_gather(shards[0], "fsdp", axis=0, tiled=True),
        lax.all_gather(shards[1], "fsdp", axis=0, tiled=True),
        lax.all_gather(shards[2], "fsdp", axis=0, tiled=True),
        lax.all_gather(shards[3], "fsdp", axis=0, tiled=True),
        lax.all_gather(shards[4], "fsdp", axis=0, tiled=True),
        lax.all_gather(shards[5], "fsdp", axis=0, tiled=True),
        lax.all_gather(shards[6], "fsdp", axis=0, tiled=True),
        lax.all_gather(shards[7], "fsdp", axis=0, tiled=True),
        lax.all_gather(shards[8], "fsdp", axis=0, tiled=True),
        lax.all_gather(shards[9], "fsdp", axis=0, tiled=True),
        lax.all_gather(shards[10], "fsdp", axis=0, tiled=True),
        lax.all_gather(shards[11], "fsdp", axis=0, tiled=True),
        lax.all_gather(shards[12], "fsdp", axis=0, tiled=True),
        lax.all_gather(shards[13], "fsdp", axis=0, tiled=True),
        lax.all_gather(shards[14], "fsdp", axis=0, tiled=True),
    )
    embedding = backward_set[0]
    first_gain = backward_set[2]
    joint = backward_set[4]
    outward = backward_set[7]
    second_gain = backward_set[9]
    expand = backward_set[11]
    shrink = backward_set[13]
    upstream = cotangent.reshape(tokens, width).astype(wide)
    upstream_low = upstream.astype(narrow)
    shrink_grad = jnp.einsum("tm,td->md", hidden, upstream_low, preferred_element_type=wide)
    shrink_offset_grad = column_sum(upstream_low)
    hidden_grad = jnp.einsum("td,md->tm", upstream_low, shrink, preferred_element_type=wide)
    upper_grad = gelu_pull(hidden_grad)[0].astype(narrow)
    expand_grad = jnp.einsum("td,tm->dm", normed_mid, upper_grad, preferred_element_type=wide)
    expand_offset_grad = column_sum(upper_grad)
    normed_mid_grad = jnp.einsum("tm,dm->td", upper_grad, expand, preferred_element_type=wide)
    second_part, second_gain_grad, second_shift_grad = norm_backward(
        normed_mid_grad, unit_second, scale_second, second_gain.astype(wide)
    )
    residual_grad = upstream + second_part
    residual_low = residual_grad.astype(narrow)
    outward_grad = jnp.einsum("te,td->ed", mixed, residual_low, preferred_element_type=wide)
    out_offset_grad = column_sum(residual_low)
    mixed_grad = jnp.einsum("td,ed->te", residual_low, outward, preferred_element_type=wide)
    mixed_grad = mixed_grad.astype(narrow).reshape(heads_shape)
    attend_wide = jnp.exp(masked_scores() - log_total)
    attend = attend_wide.astype(narrow)
    values_grad = jnp.einsum("rhqk,rqhe->rkhe", attend, mixed_grad, preferred_element_type=wide)
    attend_grad = jnp.einsum("rqhe,rkhe->rhqk", mixed_grad, values, preferred_element_type=wide)
    centered = jnp.sum(attend_grad * attend_wide, axis=-1, keepdims=True)
    scores_grad = (attend_wide * (attend_grad - centered)).astype(narrow)
    query_grad = (
        jnp.einsum("rhqk,rkhe->rqhe", scores_grad, keys, preferred_element_type=wide) * factor
    )
    keys_grad = (
        jnp.einsum("rhqk,rqhe->rkhe", scores_grad, query, preferred_element_type=wide) * factor
    )
    projected_grad = jnp.concatenate(
        [
            query_grad.reshape(tokens, width),
            keys_grad.reshape(tokens, width),
            values_grad.reshape(tokens, width),
        ],
        axis=1,
    ).astype(narrow)
    joint_grad = jnp.einsum("td,tj->dj", normed, projected_grad, preferred_element_type=wide)
    query_offset_grad = column_sum(projected_grad[:, :width])
    value_offset_grad = column_sum(projected_grad[:, 2 * width :])
    normed_grad = jnp.einsum("tj,dj->td", projected_grad, joint, preferred_element_type=wide)
    first_part, first_gain_grad, first_shift_grad = norm_backward(
        normed_grad, unit_first, scale_first, first_gain.astype(wide)
    )
    embedded_low = (residual_grad + first_part).astype(narrow)
    embedding_grad = jnp.einsum("ts,td->sd", inputs, embedded_low, preferred_element_type=wide)
    embed_offset_grad = column_sum(embedded_low)
    stem_gradient = jnp.einsum("td,sd->ts", embedded_low, embedding, preferred_element_type=wide)
    stem_gradient = stem_gradient.astype(narrow).reshape(rows, row_len, stem_width)
    terms = (
        embedding_grad,
        embed_offset_grad,
        first_gain_grad,
        first_shift_grad,
        joint_grad,
        query_offset_grad,
        value_offset_grad,
        outward_grad,
        out_offset_grad,
        second_gain_grad,
        second_shift_grad,
        expand_grad,
        expand_offset_grad,
        shrink_grad,
        shrink_offset_grad,
    )
    owned = (
        lax.psum_scatter(terms[0], "fsdp", scatter_dimension=0, tiled=True),
        lax.psum_scatter(terms[1], "fsdp", scatter_dimension=0, tiled=True),
        lax.psum_scatter(terms[2], "fsdp", scatter_dimension=0, tiled=True),
        lax.psum_scatter(terms[3], "fsdp", scatter_dimension=0, tiled=True),
        lax.psum_scatter(terms[4], "fsdp", scatter_dimension=0, tiled=True),
        lax.psum_scatter(terms[5], "fsdp", scatter_dimension=0, tiled=True),
        lax.psum_scatter(terms[6], "fsdp", scatter_dimension=0, tiled=True),
        lax.psum_scatter(terms[7], "fsdp", scatter_dimension=0, tiled=True),
        lax.psum_scatter(terms[8], "fsdp", scatter_dimension=0, tiled=True),
        lax.psum_scatter(terms[9], "fsdp", scatter_dimension=0, tiled=True),
        lax.psum_scatter(terms[10], "fsdp", scatter_dimension=0, tiled=True),
        lax.psum_scatter(terms[11], "fsdp", scatter_dimension=0, tiled=True),
        lax.psum_scatter(terms[12], "fsdp", scatter_dimension=0, tiled=True),
        lax.psum_scatter(terms[13], "fsdp", scatter_dimension=0, tiled=True),
        lax.psum_scatter(terms[14], "fsdp", scatter_dimension=0, tiled=True),
    )
    summed = lax.psum(
        (
            owned[0],
            owned[1],
            owned[2],
            owned[3],
            owned[4],
            owned[5],
            owned[6],
            owned[7],
            owned[8],
            owned[9],
            owned[10],
            owned[11],
            owned[12],
            owned[13],
            owned[14],
        ),
        "dp",
    )
    return (activations, stem_gradient) + tuple(summed)


def solution(mesh):
    in_specs = (
        P(("dp", "fsdp"), None, None),
        P(("dp", "fsdp"), None),
        P("fsdp", None),
        P("fsdp"),
        P("fsdp"),
        P("fsdp"),
        P("fsdp", None),
        P("fsdp"),
        P("fsdp"),
        P("fsdp", None),
        P("fsdp"),
        P("fsdp"),
        P("fsdp"),
        P("fsdp", None),
        P("fsdp"),
        P("fsdp", None),
        P("fsdp"),
        P(("dp", "fsdp"), None, None),
    )
    out_specs = (
        P(("dp", "fsdp"), None, None),
        P(("dp", "fsdp"), None, None),
        P("fsdp", None),
        P("fsdp"),
        P("fsdp"),
        P("fsdp"),
        P("fsdp", None),
        P("fsdp"),
        P("fsdp"),
        P("fsdp", None),
        P("fsdp"),
        P("fsdp"),
        P("fsdp"),
        P("fsdp", None),
        P("fsdp"),
        P("fsdp", None),
        P("fsdp"),
    )
    return jax.shard_map(local, mesh=mesh, in_specs=in_specs, out_specs=out_specs, check_vma=False)
```

profile of v0, /device:TPU:0, one launch (start us, length us, event | category | flops | bytes accessed | tf_op | source)
XLA Modules:
  0.0 1059.8 jit_solution(5234094786277832493)
XLA Ops:
  20.8 39.8 %all-reduce.22 = (bf16[768]{0:T(1024)(128)(2,1)S(1)}, bf16[768]{0:T(1024)(128)(2,1)S(1)}, bf16[768]{0:T(1024)(128)(2,1)S(1)}, bf16[768]{0:T(1024)(128)(2,1)S(1)}...) all-reduce(bf16[768]{0:T(1024)(128)(2,1)S(1)} %dynamic-update-slice, ...), channel_id=1, replica_groups=mesh['dp'=4,'fsdp'=8] {'fsdp'}, use_global_device_ids=true, to_apply=%add | all-reduce | flops 6912 | bytes 27648
  63.4 26.0 %all-gather = bf16[8,1,384]{2,1,0:T(2,128)(2,1)S(1)} all-gather(bf16[1,1,384]{2,1,0:T(2,128)(2,1)S(1)} %reshape.345), channel_id=1, replica_groups=mesh['dp'=4,'fsdp'=8] {'fsdp'}, dimensions={0}, use_global_device_ids=true | all-gather | bytes 6912 | tf_op jit(solution)/shard_map/all_gather | solution.py:93
  93.4 30.4 %all-gather.9.cloned.1.call-done = bf16[768,2304]{1,0:T(8,128)(2,1)} async-done(((bf16[96,2304]{1,0:T(8,128)(2,1)}), bf16[768,2304]{1,0:T(8,128)(2,1)}) %all-gather.9.cloned.1.call-update) | async-done | bytes 3538960 | tf_op jit(solution)/shard_map/all_gather | solution.py:85
  123.8 4.4 add_convert_fusion.1
  135.9 7.8 fusion.40
  143.7 8.6 fusion
  152.3 10.3 fusion.12
  162.6 2.9 all-gather.11.cloned.1.call-done
  165.6 3.1 fusion.41
  169.1 77.2 %all-gather.13.cloned.1.call-done = bf16[768,3072]{1,0:T(8,128)(2,1)} async-done(((bf16[96,3072]{1,0:T(8,128)(2,1)}), bf16[768,3072]{1,0:T(8,128)(2,1)}) %all-gather.13.cloned.1.call-update) | async-done | bytes 4718608 | tf_op jit(solution)/shard_map/all_gather | solution.py:92
  246.3 22.2 %multiply_convert_fusion.1 = (bf16[576,3072]{1,0:T(8,128)(2,1)}, f32[576,3072]{1,0:T(8,128)}, f32[576,3072]{1,0:T(8,128)}) fusion(f32[3072]{0:T(1024)S(1)} %bitcast.99, bf16[768,3072]{1,0:T(8,128)(2,1)} %all-gather.13.cloned.1.call-done, f32[576,768]{1,0:T(8,128)S(1)} %get-tuple-element.144, f32[768]{0:T(1024)S(1)} %copy-done.21, f32[768]{0:T(1024)S(1)} %copy-done.20, ...), kind=kOutput, calls=%fused_computation.15 | convolution fusion | flops 2836905984 | bytes 24205824 | tf_op jit(solution)/shard_map/dot_general | solution.py:149
  268.5 57.8 %all-gather.15.cloned.1.call-done = bf16[3072,768]{1,0:T(8,128)(2,1)} async-done(((bf16[384,768]{1,0:T(8,128)(2,1)}), bf16[3072,768]{1,0:T(8,128)(2,1)}) %all-gather.15.cloned.1.call-update) | async-done | bytes 4718608 | tf_op jit(solution)/shard_map/all_gather | solution.py:94
  326.4 10.4 convert_reduce_fusion
  336.8 3.3 multiply_reduce_fusion.1
  344.8 3.6 convolution_convert_fusion.1
  350.9 16.4 %multiply_reduce_fusion = (f32[12,576]{1,0:T(8,128)S(1)}, f32[12,576,576]{1,2,0:T(8,128)}) fusion(f32[12,576,576]{1,2,0:T(8,128)} %get-tuple-element.142, f32[12,576]{1,0:T(8,128)S(1)} %log_add_fusion, bf16[576,12,64]{0,2,1:T(8,128)(2,1)} %bitcast.85, bf16[576,12,64]{0,2,1:T(8,128)(2,1)} %bitcast.91), kind=kOutput, calls=%fused_computation.1 | convolution fusion | flops 521544960 | bytes 33675264 | tf_op jit(solution)/shard_map/rqhe,rkhe->rhqk/dot_general | solution.py:201
  367.2 12.7 %multiply_convert_fusion = bf16[12,576,576]{1,2,0:T(8,128)(2,1)S(1)} fusion(f32[12,576,576]{1,2,0:T(8,128)} %get-tuple-element.148, f32[12,576,576]{1,2,0:T(8,128)} %get-tuple-element.142, f32[12,576]{1,0:T(8,128)S(1)} %get-tuple-element.147, f32[12,576]{1,0:T(8,128)S(1)} %log_add_fusion), kind=kLoop, calls=%fused_computation | loop fusion | flops 15925248 | bytes 39868416 | tf_op jit(solution)/shard_map/convert_element_type | solution.py:203
  384.4 9.3 fusion.13
  393.8 5.6 multiply_reduce_fusion.2
  401.1 3.1 convolution_bitcast_fusion
  404.4 8.5 fusion.18
  413.0 8.6 fusion.34
  421.7 9.8 fusion.22
  431.5 64.5 %reduce-scatter.6.cloned.1.call-done = f32[128,768]{0,1:T(8,128)} async-done(((f32[1024,768]{0,1:T(8,128)}), f32[128,768]{0,1:T(8,128)}) %reduce-scatter.6.cloned.1.call-update) | async-done | bytes 393232 | tf_op jit(solution)/shard_map/reduce_scatter | solution.py:248
  496.1 131.9 %reduce-scatter.8.cloned.1.call-done = f32[96,2304]{1,0:T(8,128)} async-done(((f32[768,2304]{1,0:T(8,128)}), f32[96,2304]{1,0:T(8,128)}) %reduce-scatter.8.cloned.1.call-update) | async-done | bytes 884752 | tf_op jit(solution)/shard_map/reduce_scatter | solution.py:252
  628.0 166.6 %reduce-scatter.12.cloned.1.call-done = f32[96,3072]{1,0:T(8,128)} async-done(((f32[768,3072]{1,0:T(8,128)}), f32[96,3072]{1,0:T(8,128)}) %reduce-scatter.12.cloned.1.call-update) | async-done | bytes 1179664 | tf_op jit(solution)/shard_map/reduce_scatter | solution.py:259
  794.6 166.3 %reduce-scatter.14.cloned.1.call-done = f32[384,768]{1,0:T(8,128)} async-done(((f32[3072,768]{1,0:T(8,128)}), f32[384,768]{1,0:T(8,128)}) %reduce-scatter.14.cloned.1.call-update) | async-done | bytes 1179664 | tf_op jit(solution)/shard_map/reduce_scatter | solution.py:261
  965.0 35.7 %all-reduce.19 = (f32[768]{0:T(1024)S(1)}, f32[768]{0:T(1024)S(1)}, f32[768]{0:T(1024)S(1)}, f32[768]{0:T(1024)S(1)}, f32[768]{0:T(1024)S(1)}, /*index=5*/f32[76...) all-reduce(f32[768]{0:T(1024)S(1)} %get-tuple-element.129, ...), channel_id=3, replica_groups=mesh['dp'=4,'fsdp'=8] {'fsdp'}, use_global_device_ids=true, to_apply=%region_16.17.clone | all-reduce | flops 9984 | bytes 79872
  1001.5 6.6 all-reduce.20
  1008.0 4.0 fusion.16
  1012.1 6.4 fusion.17
  1018.5 26.6 %all-reduce.25.cloned.1.call-done = (f32[128,768]{0,1:T(8,128)}, f32[96,2304]{1,0:T(8,128)}, f32[96,768]{1,0:T(8,128)}, f32[96,3072]{1,0:T(8,128)}, f32[384,768]{1,0:T(8,128)}) async-done(((f32[128,768]{0,1:T(8,128)}, f32[96,2304]{1,0:T(8,128)}, f32[96,768]{1,0:T(8,128)}, f32[96,3072]{1,0:T(8,128)}, f32[384,768]{1,0:T(8,128)}), (f32[128,768]{0,1:T(8,128)}, f32[96,2304]{1,0:T(8,128)}, f32[96,768]{1,0:T(8,128)}, ...) | async-done | bytes 3932176 | tf_op jit(solution)/shard_map/psum | solution.py:264
  (165 shorter events, 52.6 us)
Async XLA Ops:
  7.2 83.2 %copy-start = (bf16[1,576,1024]{2,1,0:T(8,128)(2,1)S(1)}, bf16[1,576,1024]{2,1,0:T(8,128)(2,1)}, u32[]{:S(2)}) copy-start(bf16[1,576,1024]{2,1,0:T(8,128)(2,1)} %param.18) | copy-start | bytes 3538948
  7.2 83.2 %all-gather.7.cloned.1.call-start = ((), (), s32[]{:S(2)}) async-start(), calls=%async_computation.5 | async-start | bytes 1769472 | tf_op jit(solution)/shard_map/all_gather | solution.py:81
  7.9 115.9 %all-gather.9.cloned.1.call-start = ((), (), s32[]{:S(2)}) async-start(), calls=%async_computation.6 | async-start | bytes 3981312 | tf_op jit(solution)/shard_map/all_gather | solution.py:85
  8.7 156.9 %all-gather.11.cloned.1.call-start = ((), (), s32[]{:S(2)}) async-start(), calls=%async_computation.7 | async-start | bytes 1327104 | tf_op jit(solution)/shard_map/all_gather | solution.py:88
  9.4 236.9 %all-gather.13.cloned.1.call-start = ((), (), s32[]{:S(2)}) async-start(), calls=%async_computation.8 | async-start | bytes 5308416 | tf_op jit(solution)/shard_map/all_gather | solution.py:92
  10.0 316.4 %all-gather.15.cloned.1.call-start = ((), (), s32[]{:S(2)}) async-start(), calls=%async_computation.9 | async-start | bytes 5308416 | tf_op jit(solution)/shard_map/all_gather | solution.py:94
  10.6 420.9 %reduce-scatter.10.cloned.1.call-start = ((), (), s32[]{:S(2)}) async-start(), calls=%async_computation.12 | async-start | bytes 2654208 | tf_op jit(solution)/shard_map/reduce_scatter | solution.py:255
  61.6 62.2 %copy-start.24 = (f32[768]{0:T(1024)}, f32[768]{0:T(1024)S(1)}, u32[]{:S(2)}) copy-start(f32[768]{0:T(1024)S(1)} %convert_element_type.120) | copy-start | bytes 9220
  62.2 61.6 %copy-start.29 = (f32[768]{0:T(1024)}, f32[768]{0:T(1024)S(1)}, u32[]{:S(2)}) copy-start(f32[768]{0:T(1024)S(1)} %convert_element_type.121) | copy-start | bytes 9220
  93.0 35.1 %copy-start.8 = (f32[576,768]{1,0:T(8,128)}, f32[576,768]{1,0:T(8,128)S(1)}, u32[]{:S(2)}) copy-start(f32[576,768]{1,0:T(8,128)S(1)} %get-tuple-element.140) | copy-start | bytes 5308420
  93.0 35.1 %copy-start.22 = (f32[576]{0:T(1024)}, f32[576]{0:T(1024)S(1)}, u32[]{:S(2)}) copy-start(f32[576]{0:T(1024)S(1)} %broadcast_multiply_fusion.5) | copy-start | bytes 6916
  93.4 34.8 %copy-start.26 = (f32[576]{0:T(1024)}, f32[576]{0:T(1024)S(1)}, u32[]{:S(2)}) copy-start(f32[576]{0:T(1024)S(1)} %add_rsqrt_fusion.1) | copy-start | bytes 6916
  131.5 12.2 %copy-start.3 = (bf16[576,768]{0,1:T(8,128)(2,1)}, bf16[576,768]{0,1:T(8,128)(2,1)S(1)}, u32[]{:S(2)}) copy-start(bf16[576,768]{0,1:T(8,128)(2,1)S(1)} %copy.68) | copy-start | bytes 2654212
  133.4 10.3 copy-start.6
  152.3 13.3 %copy-start.31 = (f32[768]{0:T(1024)S(1)}, f32[768]{0:T(1024)}, u32[]{:S(2)}) copy-start(f32[768]{0:T(1024)} %convert_element_type.131) | copy-start | bytes 9220
  165.6 80.7 %copy-start.20 = (f32[768]{0:T(1024)S(1)}, f32[768]{0:T(1024)}, u32[]{:S(2)}) copy-start(f32[768]{0:T(1024)} %convert_element_type.132) | copy-start | bytes 9220
  165.6 80.7 %copy-start.21 = (f32[768]{0:T(1024)S(1)}, f32[768]{0:T(1024)}, u32[]{:S(2)}) copy-start(f32[768]{0:T(1024)} %convert_element_type.133) | copy-start | bytes 9220
  165.6 80.7 %copy-start.28 = (f32[8,1,384]{2,1,0:T(1,128)S(1)}, f32[8,1,384]{2,1,0:T(1,128)}, u32[]{:S(2)}) copy-start(f32[8,1,384]{2,1,0:T(1,128)} %convert_element_type.152) | copy-start | bytes 36868
  326.4 10.4 copy-start.33
  350.8 145.3 %reduce-scatter.6.cloned.1.call-start = ((), (), s32[]{:S(2)}) async-start(), calls=%async_computation.10 | async-start | bytes 3538944 | tf_op jit(solution)/shard_map/reduce_scatter | solution.py:248
  367.2 12.7 %copy-start.4 = (bf16[576,768]{0,1:T(8,128)(2,1)S(1)}, bf16[576,768]{0,1:T(8,128)(2,1)}, u32[]{:S(2)}) copy-start(bf16[576,768]{0,1:T(8,128)(2,1)} %copy-done.3) | copy-start | bytes 2654212
  381.7 12.1 %copy-start.10 = (bf16[12,64,576]{2,1,0:T(8,128)(2,1)}, bf16[12,64,576]{2,1,0:T(8,128)(2,1)S(1)}, u32[]{:S(2)}) copy-start(bf16[12,64,576]{2,1,0:T(8,128)(2,1)S(1)} %multiply_convert_fusion.3) | copy-start | bytes 2654212
  384.4 9.3 copy-start.17
  384.4 9.3 copy-start.9
  384.4 9.3 copy-start.23
  384.4 9.3 copy-start.25
  384.4 9.3 copy-start.27
  404.1 223.9 %reduce-scatter.8.cloned.1.call-start = ((), (), s32[]{:S(2)}) async-start(), calls=%async_computation.11 | async-start | bytes 7962624 | tf_op jit(solution)/shard_map/reduce_scatter | solution.py:252
  412.9 381.6 %reduce-scatter.12.cloned.1.call-start = ((), (), s32[]{:S(2)}) async-start(), calls=%async_computation.13 | async-start | bytes 10616832 | tf_op jit(solution)/shard_map/reduce_scatter | solution.py:259
  421.6 539.3 %reduce-scatter.14.cloned.1.call-start = ((), (), s32[]{:S(2)}) async-start(), calls=%async_computation.14 | async-start | bytes 10616832 | tf_op jit(solution)/shard_map/reduce_scatter | solution.py:261
  431.5 530.7 %copy-start.32 = (bf16[768]{0:T(1024)(128)(2,1)S(1)}, bf16[768]{0:T(1024)(128)(2,1)}, u32[]{:S(2)}) copy-start(bf16[768]{0:T(1024)(128)(2,1)} %get-tuple-element.126) | copy-start | bytes 4612
  431.5 613.6 %all-reduce.25.cloned.1.call-start = ((), (), s32[]{:S(2)}) async-start(), calls=%async_computation.15 | async-start | bytes 7864320 | tf_op jit(solution)/shard_map/psum | solution.py:264
  (14 other events, 55.7 us)
Sparse Core Ops, SparseCore 0:
  10.2 47.0 all-gather.6
  59.5 64.2 all-gather.8
  126.0 39.5 all-gather.10
  167.6 78.6 all-gather.12
  248.3 78.0 all-gather.14
  350.9 67.2 reduce-scatter.9
  421.9 74.1 reduce-scatter.5
  499.8 128.1 reduce-scatter.7
  632.0 162.4 reduce-scatter.11
  798.4 162.3 reduce-scatter.13
  963.8 81.2 all-reduce.24
where the time goes:
time: 1070 us; the launch traced here: 1060 us
  waiting for transfers between devices  727 us (68%)
  matrix products  146 us (14%)
  blocking collectives  108 us (10%)
  local copies, waits for them, and re-layouts  30.6 us (3%)
  other arithmetic  29.9 us (3%)
  between operations  16.7 us (2%)
    reduce_scatter x1, waiting for transfers between devices, local(): lax.psum_scatter(terms[11], 'fsdp', scatter_dimension=0, tiled=True)  167 us
    reduce_scatter x1, waiting for transfers between devices, local(): lax.psum_scatter(terms[13], 'fsdp', scatter_dimension=0, tiled=True)  166 us
    reduce_scatter x1, waiting for transfers between devices, local(): lax.psum_scatter(terms[4], 'fsdp', scatter_dimension=0, tiled=True)  132 us
    all_gather x1, waiting for transfers between devices, local(): lax.all_gather(shards[11], 'fsdp', axis=0, tiled=True)  77.2 us
    unnamed x2, blocking collectives  75.5 us
    reduce_scatter x1, waiting for transfers between devices, local(): lax.psum_scatter(terms[0], 'fsdp', scatter_dimension=0, tiled=True)  64.5 us
    all_gather x1, waiting for transfers between devices, local(): lax.all_gather(shards[13], 'fsdp', axis=0, tiled=True)  57.8 us
    all_gather x1, waiting for transfers between devices, local(): lax.all_gather(shards[4], 'fsdp', axis=0, tiled=True)  30.4 us
  transfers between devices with their start and end apart: 11, of which 9 were waited for; matrix products, arithmetic and copies ran while one was open for 16% of the time, Pallas kernels for 0%

commit v1 on v0

--- a/solution.py
+++ b/solution.py
@@ -1,12 +1,956 @@
 import math
+import types
 
 import jax
 import jax.numpy as jnp
 from jax import lax
+from jax.experimental import pallas as pl
+from jax.experimental.pallas import tpu as pltpu
 from jax.sharding import PartitionSpec as P
 
 HEADS = 12
 HEAD_DIM = 64
+AXIS = "fsdp"
+MESH = pl.DeviceIdType.MESH
+WIDE = jnp.float32
+NARROW = jnp.bfloat16
+
+EMBED_BIAS, FIRST_GAIN, FIRST_SHIFT, QUERY_BIAS, VALUE_BIAS, OUT_BIAS = 0, 1, 2, 3, 4, 5
+SECOND_GAIN, SECOND_SHIFT, SHRINK_BIAS, EXPAND_BIAS = 6, 7, 8, 9
+VECTOR_ROWS = 16
+
+EMBED, JOINT, OUT, EXPAND, SHRINK = 0, 1, 2, 3, 4
+
+ORDER = (
+    32, 33, 34, 35, 64, 65, 66, 0, 96, 544, 128, 97, 129, 98, 130, 545, 0, 99, 131, 160,
+    36, 67, 68, 69, 70, 161, 37, 71, 162, 38, 72, 163, 39, 73, 100, 132, 192, 101, 133, 164,
+    40, 74, 102, 134, 224, 165, 41, 75, 103, 135, 193, 256, 0, 166, 42, 76, 194, 167, 43, 77,
+    225, 104, 136, 288, 195, 257, 0, 226, 0, 168, 44, 78, 105, 137, 258, 0, 106, 227, 138, 289,
+    196, 169, 45, 79, 107, 139, 170, 46, 259, 0, 290, 108, 171, 47, 140, 197, 228, 172, 291, 109,
+    260, 141, 0, 198, 0, 110, 173, 199, 229, 142, 111, 143, 0, 292, 0, 174, 261, 175, 230, 200,
+    0, 0, 231, 262, 0, 201, 293, 0, 263, 232, 0, 202, 294, 203, 0, 233, 264, 204, 0, 234,
+    295, 0, 205, 265, 235, 0, 266, 206, 207, 236, 296, 0, 267, 237, 0, 268, 297, 0, 238, 269,
+    239, 298, 0, 320, 321, 322, 299, 0, 300, 270, 271, 0, 301, 352, 0, 353, 302, 0, 354, 303,
+    0, 0, 384, 0, 385, 0, 323, 0, 324, 386, 0, 325, 355, 416, 0, 326, 356, 0, 357, 358,
+    0, 0, 327, 387, 417, 0, 448, 0, 359, 388, 0, 418, 0, 389, 449, 0, 419, 0, 0, 328,
+    390, 0, 329, 480, 0, 330, 0, 360, 450, 481, 361, 423, 362, 512, 0, 451, 420, 392, 513, 0,
+    482, 0, 0, 393, 421, 455, 0, 331, 394, 514, 0, 332, 483, 0, 333, 422, 363, 487, 0, 452,
+    364, 424, 365, 515, 519, 425, 0, 334, 395, 0, 335, 453, 484, 426, 0, 336, 366, 396, 0, 0,
+    367, 427, 368, 454, 397, 577, 485, 516, 428, 456, 398, 578, 399, 457, 517, 429, 400, 579, 458, 486,
+    488, 430, 489, 580, 459, 490, 518, 431, 520, 581, 460, 521, 491, 522, 432, 461, 492, 523, 462, 493,
+    524, 463, 494, 525, 464, 495, 526, 496, 527, 528,
+)
+
+
+def nn(left, right):
+    return lax.dot_general(left, right, (((1,), (0,)), ((), ())), preferred_element_type=WIDE)
+
+
+def nt(left, right):
+    return lax.dot_general(left, right, (((1,), (1,)), ((), ())), preferred_element_type=WIDE)
+
+
+def tn(left, right):
+    return lax.dot_general(left, right, (((0,), (0,)), ((), ())), preferred_element_type=WIDE)
+
+
+def aligned(value, step):
+    return pl.multiple_of(value, step)
+
+
+def gelu_pair(upper):
+    cdf = 0.5 * (1.0 + lax.erf(upper * (1.0 / math.sqrt(2.0))))
+    density = jnp.exp(-0.5 * upper * upper) * (1.0 / math.sqrt(2.0 * math.pi))
+    return upper * cdf, cdf + upper * density
+
+
+def gather_split(rows):
+    half = rows // 2
+    share = 16 * max(1, (half * 5) // 192)
+    return share, half - 2 * share
+
+
+def reduce_split(weight, rows):
+    half = rows // 2
+    share = 0 if weight == OUT else 16 * max(1, half // 64)
+    return share, half - 2 * share
+
+
+def column_chunks(width, step):
+    return [(start, step) for start in range(0, width, step)]
+
+
+def fused_kernel(tokens, width, stem_width, mlp, sizes, gather_plan, reduce_plan, names, *refs):
+    vec_in, lengths, stem_hbm, cot_hbm = refs[:4]
+    shard, (act_hbm, stem_grad_hbm) = refs[4:9], refs[9:11]
+    result, vec_out = refs[11:16], refs[16]
+    ref = types.SimpleNamespace(**dict(zip(names, refs[17:])))
+    full = ref.full
+    local_grad = [ref.core_shrink] + list(full[1:4]) + [ref.shrink_grad]
+    resid, work, bias = ref.resid, ref.work, ref.bias
+    unit1, unit2, scale1, scale2 = ref.unit1, ref.unit2, ref.scale1, ref.scale2
+    normed, normed_mid, proj = ref.normed, ref.normed_mid, ref.proj
+    mixed_t, mixed, lse, delta = ref.mixed_t, ref.mixed, ref.lse, ref.delta
+    pull, hidden, cot, stem, low = ref.pull, ref.hidden, ref.cot, ref.stem, ref.low
+    vecs, vec_all, vec_sum = ref.vecs, ref.vec_all, ref.vec_sum
+    fold = ref.fold
+
+    dp, fs = lax.axis_index("dp"), lax.axis_index(AXIS)
+    y, c = lax.div(dp, 2), lax.rem(dp, 2)
+    z, x = lax.div(fs, 2), lax.rem(fs, 2)
+    z_others = (z + 1 - 2 * lax.rem(z, 2), lax.rem(z + 2, 4), 3 - z)
+    at_core = (y * 2 + 1 - c, fs)
+    at_y = ((1 - y) * 2 + c, fs)
+    at_x = (dp, z * 2 + 1 - x)
+    at_z = tuple((dp, other * 2 + x) for other in z_others)
+
+    def send(src, dst, send_sem, recv_sem, where):
+        return pltpu.make_async_remote_copy(
+            src_ref=src,
+            dst_ref=dst,
+            send_sem=send_sem,
+            recv_sem=recv_sem,
+            device_id=where,
+            device_id_type=MESH,
+        )
+
+
+    up = lax.div(z, 2)
+    inner = (z == 1) | (z == 2)
+    arrivals = (z_others[0], 2 - up, 3 - 3 * up)
+    fill, g_send, g_recv = ref.fill, ref.g_send, ref.g_recv
+
+    def gather_refs(k):
+        weight, start, count = gather_plan[k]
+        rows = sizes[weight][0]
+        half = rows // 2
+        share, both = gather_split(rows)
+        mine = pl.ds(aligned(c * half + y * share, 16), share + both)
+        passed = pl.ds(aligned(c * half + y * (share + both), 16), share)
+        halves = pl.ds(aligned(c * half, 16), half)
+        return full[weight], shard[weight], mine, passed, halves, pl.ds(start, count)
+
+    def fill_copy(k):
+        whole, own, _, _, halves, cols = gather_refs(k)
+        return pltpu.make_async_copy(own.at[halves, cols], whole.at[z, x, halves, cols], fill.at[k])
+
+    def own_copy(k, sent, got, where):
+        whole, own, mine, _, _, cols = gather_refs(k)
+        return send(own.at[mine, cols], whole.at[z, x, mine, cols], g_send.at[sent, k], g_recv.at[got, k], where)
+
+    def same_copy(part, k, sent, got, where):
+        return send(part, part, g_send.at[sent, k], g_recv.at[got, k], where)
+
+    def z_copy(k, order, sent, got, where):
+        whole, _, mine, _, _, cols = gather_refs(k)
+        return same_copy(whole.at[arrivals[order], x, mine, cols], k, sent, got, where)
+
+    def across(k):
+        return (z_copy(k, 0, 2, 2, at_z[2]), z_copy(k, 1, 3, 1, at_z[0]), z_copy(k, 2, 4, 2, at_z[0]))
+
+    def x_copy(k, order):
+        whole, _, mine, _, _, cols = gather_refs(k)
+        return same_copy(whole.at[arrivals[order], x, mine, cols], k, 5, 5, at_x)
+
+    def x_bytes(k):
+        whole, _, mine, _, _, cols = gather_refs(k)
+        return same_copy(whole.at[:, x, mine, cols], k, 5, 5, at_x)
+
+    def y_copy(k, order):
+        whole, _, _, passed, _, cols = gather_refs(k)
+        return same_copy(whole.at[arrivals[order], x, passed, cols], k, 6, 6, at_y)
+
+    def y_bytes(k):
+        whole, _, _, passed, _, cols = gather_refs(k)
+        return same_copy(whole.at[pl.ds(0, 3), x, passed, cols], k, 6, 6, at_y)
+
+    def y_copy_late(k):
+        whole, _, _, passed, _, cols = gather_refs(k)
+        return same_copy(whole.at[:, 1 - x, passed, cols], k, 7, 7, at_y)
+
+    def core_copy(k):
+        whole, _, _, _, halves, cols = gather_refs(k)
+        return same_copy(whole.at[:, :, halves, cols], k, 8, 8, at_core)
+
+    def start_z(k):
+        own_copy(k, 0, 0, at_z[0]).start()
+
+        @pl.when(inner)
+        def _():
+            own_copy(k, 1, 1, at_z[2]).start()
+
+        fill_copy(k).start()
+
+    def start_x(k):
+        own_copy(k, 5, 5, at_x).start()
+
+    def gather_z(order):
+        def step(k):
+            z_copy(k, order, order, order, at_z[0]).wait_recv()
+
+            @pl.when(inner)
+            def _():
+                across(k)[order].start()
+
+            x_copy(k, order).start()
+            y_copy(k, order).start()
+
+        return step
+
+    def gather_x(k):
+        x_bytes(k).wait_recv()
+        y_copy_late(k).start()
+
+    def gather_y(k):
+        fill_copy(k).wait()
+        y_bytes(k).wait_recv()
+        y_copy_late(k).wait_recv()
+        core_copy(k).start()
+
+    def gather_core(k):
+        core_copy(k).wait_recv()
+
+    def gather_sent(k):
+        own_copy(k, 0, 0, at_z[0]).wait_send()
+
+        @pl.when(inner)
+        def _():
+            own_copy(k, 1, 1, at_z[2]).wait_send()
+            for copy in across(k):
+                copy.wait_send()
+
+        x_bytes(k).wait_send()
+        y_bytes(k).wait_send()
+        y_copy_late(k).wait_send()
+        core_copy(k).wait_send()
+
+    r_send, r_recv, r_done = ref.r_send, ref.r_recv, ref.r_done
+    from_y, from_x, from_z = ref.from_y, ref.from_x, ref.from_z
+    part_out, part_in, final = ref.part_out, ref.part_in, ref.final
+    free = ref.free
+
+    def core_slot(k):
+        weight, start, count = reduce_plan[k]
+        if weight == SHRINK:
+            return ref.core_shrink.at[:, :, :, pl.ds(start, count)]
+        if weight == EMBED:
+            return ref.core_embed.at[:, :, :, pl.ds(start, count)]
+        half = sizes[weight][0] // 2
+        before = {EXPAND: 0, OUT: mlp // width, JOINT: mlp // width + 1}[weight]
+        return full[SHRINK].at[:, :, pl.ds((before + start // width) * half, half), pl.ds(start % width, count)]
+
+    def reduce_refs(k):
+        weight, start, count = reduce_plan[k]
+        share, both = reduce_split(weight, sizes[weight][0])
+        return weight, sizes[weight][0] // 2, share, both, pl.ds(start, count)
+
+    def r1_copy(k):
+        weight, half, _, _, cols = reduce_refs(k)
+        src = local_grad[weight].at[:, :, pl.ds(aligned((1 - c) * half, 16), half), cols]
+        return send(src, core_slot(k), r_send.at[0, k], r_recv.at[0, k], at_core)
+
+    def r2_copy(k):
+        weight, half, share, both, cols = reduce_refs(k)
+        rows = pl.ds(aligned(c * half + (1 - y) * (share + both), 16), share)
+        return send(
+            local_grad[weight].at[:, :, rows, cols],
+            from_y[weight].at[:, :, :, cols],
+            r_send.at[1, k],
+            r_recv.at[1, k],
+            at_y,
+        )
+
+    def mine_rows(half, share, both):
+        return pl.ds(aligned(c * half + y * share, 16), share + both)
+
+    def r3_copy(k):
+        weight, half, share, both, cols = reduce_refs(k)
+        return send(
+            local_grad[weight].at[:, 1 - x, mine_rows(half, share, both), cols],
+            from_x[weight].at[:, :, cols],
+            r_send.at[2, k],
+            r_recv.at[2, k],
+            at_x,
+        )
+
+    def r4_copy(k, j):
+        weight, half, share, both, cols = reduce_refs(k)
+        return send(
+            local_grad[weight].at[z_others[j], x, mine_rows(half, share, both), cols],
+            from_z[weight].at[j, :, cols],
+            r_send.at[3, k],
+            r_recv.at[3, k],
+            at_z[j],
+        )
+
+    def r4_bytes(k):
+        weight, _, _, _, cols = reduce_refs(k)
+        part = from_z[weight].at[:, :, cols]
+        return send(part, part, r_send.at[3, k], r_recv.at[3, k], at_z[0])
+
+    def r5_copy(k):
+        weight, _, _, _, cols = reduce_refs(k)
+        return send(
+            part_out[weight].at[:, cols], part_in[weight].at[:, cols], r_send.at[4, k], r_recv.at[4, k], at_y
+        )
+
+    def r6_copies(k):
+        weight, half, _, _, cols = reduce_refs(k)
+        rows = pl.ds(aligned(c * half, 16), half)
+        src, dst = final[weight].at[:, cols], result[weight].at[rows, cols]
+        return (
+            send(src, dst, r_send.at[5, k], r_recv.at[5, k], at_core),
+            pltpu.make_async_copy(src, dst, r_done.at[k]),
+        )
+
+    def r6_incoming(k):
+        weight, half, _, _, cols = reduce_refs(k)
+        rows = pl.ds(aligned((1 - c) * half, 16), half)
+        part = result[weight].at[rows, cols]
+        return send(part, part, r_send.at[5, k], r_recv.at[5, k], at_core)
+
+    def reduce_1(k):
+        if reduce_plan[k][:2] == (EXPAND, 0):
+            pl.semaphore_wait(free, 1)
+        r1_copy(k).start()
+
+    def reduce_2(k):
+        weight, half, share, _, cols = reduce_refs(k)
+        r1_copy(k).wait_recv()
+        slot, total = core_slot(k), local_grad[weight]
+        rows = pl.ds(aligned(c * half, 16), half)
+        for i in range(4):
+            for j in range(2):
+                total[i, j, rows, cols] = total[i, j, rows, cols] + slot[i, j]
+        if share:
+            r2_copy(k).start()
+        else:
+            r3_copy(k).start()
+
+    def reduce_3(k):
+        weight, half, share, both, cols = reduce_refs(k)
+        r2_copy(k).wait_recv()
+        total = local_grad[weight]
+        rows = pl.ds(aligned(c * half + y * (share + both), 16), share)
+        for i in range(4):
+            for j in range(2):
+                total[i, j, rows, cols] = total[i, j, rows, cols] + from_y[weight][i, j, :, cols]
+        r3_copy(k).start()
+
+    def reduce_4(k):
+        weight, half, share, both, cols = reduce_refs(k)
+        r3_copy(k).wait_recv()
+        total = local_grad[weight]
+        rows = mine_rows(half, share, both)
+        for i in range(4):
+            total[i, x, rows, cols] = total[i, x, rows, cols] + from_x[weight][i, :, cols]
+        for j in range(3):
+            r4_copy(k, j).start()
+
+    def reduce_5(k):
+        weight, half, share, both, cols = reduce_refs(k)
+        r4_bytes(k).wait_recv()
+        value = local_grad[weight][z, x, mine_rows(half, share, both), cols].astype(WIDE)
+        for j in range(3):
+            value = value + from_z[weight][j, :, cols].astype(WIDE)
+        part_out[weight][:, cols] = value.astype(NARROW)
+        r5_copy(k).start()
+
+    def reduce_6(k):
+        weight, half, share, both, cols = reduce_refs(k)
+        r5_copy(k).wait_recv()
+        own, came, whole = part_out[weight], part_in[weight], final[weight]
+
+        def rows(start, count):
+            return pl.ds(aligned(start, 16), count)
+
+        if share:
+            whole[rows(y * (share + both), share), cols] = own[rows(y * both, share), cols].astype(WIDE)
+            whole[rows((1 - y) * (share + both), share), cols] = came[rows((1 - y) * both, share), cols].astype(WIDE)
+        whole[share : share + both, cols] = own[rows((1 - y) * share, both), cols].astype(WIDE) + came[
+            rows(y * share, both), cols
+        ].astype(WIDE)
+        for copy in r6_copies(k):
+            copy.start()
+
+    def reduce_7(k):
+        r6_incoming(k).wait_recv()
+        r1_copy(k).wait_send()
+        if reduce_refs(k)[2]:
+            r2_copy(k).wait_send()
+        r3_copy(k).wait_send()
+        r4_bytes(k).wait_send()
+        r5_copy(k).wait_send()
+        remote, local = r6_copies(k)
+        remote.wait_send()
+        local.wait()
+
+    def row(place):
+        return vecs[place : place + 1, :]
+
+    def layer_norm(unit, scale, out, gain, shift):
+        def step(n, carry):
+            rows = pl.ds(aligned(n * 96, 96), 96)
+            values = resid[rows, :]
+            center = values - jnp.mean(values, axis=1, keepdims=True)
+            factor = lax.rsqrt(jnp.mean(center * center, axis=1, keepdims=True) + 1e-6)
+            units = center * factor
+            scale[rows, :] = factor
+            unit[rows, :] = units.astype(NARROW)
+            out[rows, :] = (units * row(gain) + row(shift)).astype(NARROW)
+            return carry
+
+        lax.fori_loop(0, tokens // 96, step, 0)
+
+    def eight(values):
+        return jnp.sum(values.reshape(values.shape[0] // 8, 8, values.shape[1]), axis=0)
+
+    def norm_backward(unit, scale, gain, upstream, keep_wide, places):
+        fold[...] = jnp.zeros_like(fold)
+
+        def step(n, carry):
+            rows = pl.ds(aligned(n * 96, 96), 96)
+            grads = work[rows, :]
+            units = unit[rows, :].astype(WIDE)
+            inner = grads * row(gain)
+            fold[0:8, :] += eight(grads * units)
+            fold[8:16, :] += eight(grads)
+            value = upstream[rows, :].astype(WIDE) + scale[rows, :] * (
+                inner
+                - jnp.mean(inner, axis=1, keepdims=True)
+                - units * jnp.mean(inner * units, axis=1, keepdims=True)
+            )
+            if keep_wide:
+                resid[rows, :] = value
+            narrow = value.astype(NARROW)
+            low[rows, :] = narrow
+            fold[16:24, :] += eight(narrow.astype(WIDE))
+            return carry
+
+        lax.fori_loop(0, tokens // 96, step, 0)
+        for n, place in enumerate(places):
+            vec_sum[0, place : place + 1, :] = jnp.sum(fold[8 * n : 8 * n + 8, :], axis=0, keepdims=True)
+
+    def column_sum(source, start, place, at=0, count=width):
+        def step(n, total):
+            return total + eight(source[pl.ds(aligned(n * 96, 96), 96), start : start + count].astype(WIDE))
+
+        total = lax.fori_loop(0, tokens // 96, step, jnp.zeros((8, count), WIDE))
+        vec_sum[0, place : place + 1, at : at + count] = jnp.sum(total, axis=0, keepdims=True)
+
+    lane = lax.broadcasted_iota(jnp.int32, (1, 2 * HEAD_DIM), 1)
+
+    def head_lanes(head, value):
+        return jnp.where((lane < HEAD_DIM) == (head == 0), value, 0.0).astype(NARROW)
+
+    factor = 1.0 / math.sqrt(HEAD_DIM)
+
+    def attend_forward(p):
+        def run():
+            at = p * 128
+            query = proj[:, pl.ds(at, 128)]
+            keys = proj[:, pl.ds(width + at, 128)]
+            values_t = proj[:, pl.ds(2 * width + at, 128)].T
+            for head in range(2):
+                scores = nt(keys * head_lanes(head, factor), query) + bias[...].astype(WIDE)
+                largest = jnp.max(scores, axis=0, keepdims=True)
+                expos = jnp.exp(scores - largest)
+                total = jnp.sum(expos, axis=0, keepdims=True)
+                mix = nn(values_t[64 * head : 64 * head + 64], expos.astype(NARROW)) * (1.0 / total)
+                mixed_t[pl.ds(aligned(at + 64 * head, 64), 64), :] = mix.astype(NARROW)
+                lse[pl.ds(2 * p + head, 1), :] = largest + jnp.log(total)
+
+        return run
+
+    def attend_backward(p):
+        def run():
+            at = p * 128
+            query = proj[:, pl.ds(at, 128)]
+            keys = proj[:, pl.ds(width + at, 128)]
+            values = proj[:, pl.ds(2 * width + at, 128)]
+            grads = mixed[:, pl.ds(at, 128)]
+            keys_t = keys.T
+            value_grads, key_grads = [], []
+            for head in range(2):
+                scores = nt(keys * head_lanes(head, factor), query) + bias[...].astype(WIDE)
+                attend = jnp.exp(scores - lse[pl.ds(2 * p + head, 1), :])
+                attend_grad = nt(values * head_lanes(head, 1.0), grads)
+                scores_grad = (attend * (attend_grad - delta[pl.ds(2 * p + head, 1), :])).astype(NARROW)
+                value_grads.append(nn(attend.astype(NARROW), grads))
+                key_grads.append(nn(scores_grad, query))
+                query_grad = nn(keys_t[64 * head : 64 * head + 64], scores_grad) * factor
+                mixed_t[pl.ds(aligned(at + 64 * head, 64), 64), :] = query_grad.astype(NARROW)
+            first_head = lane < HEAD_DIM
+            pull[:, pl.ds(2 * width + at, 128)] = jnp.where(first_head, *value_grads).astype(NARROW)
+            pull[:, pl.ds(width + at, 128)] = (jnp.where(first_head, *key_grads) * factor).astype(NARROW)
+
+        return run
+
+    barrier = pltpu.get_barrier_semaphore()
+    partners = (at_core, at_y, at_x) + at_z
+    for partner in partners:
+        pl.semaphore_signal(barrier, inc=1, device_id=partner, device_id_type=MESH)
+    load_stem = pltpu.make_async_copy(stem_hbm, stem, ref.load.at[0])
+    load_cot = pltpu.make_async_copy(cot_hbm, cot, ref.load.at[1])
+    load_stem.start()
+    load_cot.start()
+    pl.semaphore_wait(barrier, len(partners))
+
+    v_send, v_recv = ref.v_send, ref.v_recv
+    vec_z = [send(vec_in, vec_all.at[z, x], v_send.at[0], v_recv.at[0], at_z[j]) for j in range(3)]
+    vec_z_part = vec_all.at[pl.ds(0, 3), x]
+    vec_z_bytes = send(vec_z_part, vec_z_part, v_send.at[0], v_recv.at[0], at_z[0])
+    vec_x_part = vec_all.at[:, x]
+    vec_x = send(vec_x_part, vec_x_part, v_send.at[1], v_recv.at[1], at_x)
+    vec_all[z, x] = vec_in[...]
+    for copy in vec_z:
+        copy.start()
+
+    def vec_gather(n):
+        if n == 0:
+            vec_z_bytes.wait_recv()
+            vec_x.start()
+        else:
+            vec_x.wait_recv()
+
+    vec_from = ref.vec_from
+    vec_partners = (at_core, at_y, at_x, at_z[0], at_z[1])
+
+    def vec_copy(n):
+        return send(vec_sum.at[n], vec_from.at[n], v_send.at[2 + n], v_recv.at[2 + n], vec_partners[n])
+
+    def vec_step(n):
+        vec_copy(n - 1).wait_recv()
+        vec_sum[n] = vec_sum[n - 1] + vec_from[n - 1]
+        if n < len(vec_partners):
+            vec_copy(n).start()
+
+    blocks = []
+    block = blocks.append
+
+    @block
+    def make_bias():
+        places = lax.broadcasted_iota(jnp.int32, (1, tokens), 1)
+        places_down = lax.broadcasted_iota(jnp.int32, (tokens, 1), 0)
+        labels = jnp.zeros((1, tokens), jnp.int32)
+        labels_down = jnp.zeros((tokens, 1), jnp.int32)
+        bound = 0
+        for n in range(lengths.shape[1]):
+            bound = bound + lengths[0, n]
+            labels = labels + (places >= bound).astype(jnp.int32)
+            labels_down = labels_down + (places_down >= bound).astype(jnp.int32)
+        bias[...] = jnp.where(labels_down == labels, 0.0, -1e30).astype(NARROW)
+        vec_sum[0] = jnp.zeros((VECTOR_ROWS, width), WIDE)
+
+    @block
+    def add_vectors():
+        totals = vec_all[0, 0].astype(WIDE)
+        for i in range(4):
+            for j in range(2):
+                if i + j > 0:
+                    totals = totals + vec_all[i, j].astype(WIDE)
+        vecs[...] = totals
+        vec_z_bytes.wait_send()
+        vec_x.wait_send()
+        load_stem.wait()
+        load_cot.wait()
+
+    def chunks(plan, weight):
+        return [item[1:] for item in plan if item[0] == weight]
+
+    def embed(start, count):
+        def run():
+            piece = full[EMBED][:, :, :, start : start + count].reshape(stem_width, count)
+            offset = vecs[EMBED_BIAS : EMBED_BIAS + 1, start : start + count]
+            resid[:, start : start + count] = nn(stem[...], piece) + offset
+
+        return run
+
+    def project(start, count):
+        def run():
+            value = nn(normed[...], full[JOINT][:, :, :, start : start + count].reshape(width, count))
+            at = start % width
+            if start // width == 0:
+                value = value + vecs[QUERY_BIAS : QUERY_BIAS + 1, at : at + count]
+            if start // width == 2:
+                value = value + vecs[VALUE_BIAS : VALUE_BIAS + 1, at : at + count]
+            proj[:, start : start + count] = value.astype(NARROW)
+
+        return run
+
+    for item in chunks(gather_plan, EMBED):
+        block(embed(*item))
+
+    @block
+    def first_norm():
+        layer_norm(unit1, scale1, normed, FIRST_GAIN, FIRST_SHIFT)
+
+    for item in chunks(gather_plan, JOINT):
+        block(project(*item))
+    for p in range(HEADS // 2):
+        block(attend_forward(p))
+
+    @block
+    def join_heads():
+        mixed[...] = mixed_t[...].T
+        resid[...] = resid[...] + nn(mixed[...], full[OUT][...].reshape(width, width)) + row(OUT_BIAS)
+
+    @block
+    def second_norm():
+        layer_norm(unit2, scale2, normed_mid, SECOND_GAIN, SECOND_SHIFT)
+
+    def expand_forward(i):
+        def run():
+            start = i * width
+            work[...] = nn(normed_mid[...], full[EXPAND][:, :, :, start : start + width].reshape(width, width))
+
+            def gelu_step(n, carry):
+                rows = pl.ds(aligned(n * 64, 64), 64)
+                for at in range(0, width, 128):
+                    offset = vecs[EXPAND_BIAS + i : EXPAND_BIAS + i + 1, at : at + 128]
+                    value, slope = gelu_pair(work[rows, at : at + 128] + offset)
+                    hidden[rows, start + at : start + at + 128] = value.astype(NARROW)
+                    pull[rows, start + at : start + at + 128] = slope.astype(NARROW)
+                return carry
+
+            lax.fori_loop(0, tokens // 64, gelu_step, 0)
+
+        return run
+
+    rows_shrink = sizes[SHRINK][0]
+
+    def shrink_gradient(i):
+        def run():
+            for j in range(2):
+                at = rows_shrink * (2 * i + j)
+                local_grad[SHRINK][i, j] = tn(hidden[:, at : at + rows_shrink], cot[...]).astype(NARROW)
+
+        return run
+
+    for i in range(4):
+        block(expand_forward(i))
+        block(shrink_gradient(i))
+
+    @block
+    def cotangent_sum():
+        column_sum(cot, 0, SHRINK_BIAS)
+
+    def hidden_backward(i):
+        def run():
+            at = i * width
+            grads = nt(cot[...], full[SHRINK][i].reshape(width, width))
+            pull[:, at : at + width] = (grads * pull[:, at : at + width].astype(WIDE)).astype(NARROW)
+            column_sum(pull, at, EXPAND_BIAS + i)
+
+        return run
+
+    for i in range(4):
+        block(hidden_backward(i))
+    store_act = pltpu.make_async_copy(low, act_hbm, ref.load.at[0])
+    store_stem = pltpu.make_async_copy(hidden.at[:, pl.ds(0, stem_width)], stem_grad_hbm, ref.load.at[1])
+
+    @block
+    def activations():
+        value = nn(hidden[...], full[SHRINK][...].reshape(mlp, width))
+        low[...] = (resid[...] + value + row(SHRINK_BIAS)).astype(NARROW)
+        store_act.start()
+        pl.semaphore_signal(free, inc=1, device_id=at_core, device_id_type=MESH)
+
+    @block
+    def expand_backward():
+        work[...] = nt(pull[...], full[EXPAND][...].reshape(width, mlp))
+
+    def expand_gradient(i):
+        def run():
+            at = i * width
+            value = tn(normed_mid[...], pull[:, at : at + width]).astype(NARROW)
+            full[EXPAND][:, :, :, at : at + width] = value.reshape(4, 2, width // 8, width)
+
+        return run
+
+    for i in range(4):
+        block(expand_gradient(i))
+
+    @block
+    def second_norm_backward():
+        store_act.wait()
+        norm_backward(unit2, scale2, SECOND_GAIN, cot, True, (SECOND_GAIN, SECOND_SHIFT, OUT_BIAS))
+
+    @block
+    def out_backward():
+        mixed[...] = nt(low[...], full[OUT][...].reshape(width, width)).astype(NARROW)
+
+    @block
+    def out_gradient():
+        full[OUT][...] = nn(mixed_t[...], low[...]).astype(NARROW).reshape(4, 2, width // 8, width)
+
+    @block
+    def row_sums():
+        grads_t = mixed[...].T
+        for head in range(HEADS):
+            span = slice(64 * head, 64 * head + 64)
+            product = grads_t[span].astype(WIDE) * mixed_t[span, :].astype(WIDE)
+            delta[head : head + 1, :] = jnp.sum(product, axis=0, keepdims=True)
+
+    def gather_query(half):
+        def run():
+            at = half * width // 2
+            pull[:, at : at + width // 2] = mixed_t[at : at + width // 2, :].T
+            column_sum(pull, at, QUERY_BIAS, at, width // 2)
+            column_sum(pull, 2 * width + at, VALUE_BIAS, at, width // 2)
+
+        return run
+
+    def joint_backward(half):
+        def run():
+            total = 0.0 if half == 0 else work[...]
+            for part in range(3):
+                at = part * width + half * width // 2
+                weight = full[JOINT][:, :, :, at : at + width // 2].reshape(width, width // 2)
+                total = total + nt(pull[:, at : at + width // 2], weight)
+            work[...] = total
+
+        return run
+
+    def joint_gradient(start, count):
+        def run():
+            value = tn(normed[...], pull[:, start : start + count]).astype(NARROW)
+            full[JOINT][:, :, :, start : start + count] = value.reshape(4, 2, width // 8, count)
+
+        return run
+
+    for half in range(2):
+        for p in range(HEADS // 4):
+            block(attend_backward(half * HEADS // 4 + p))
+        block(gather_query(half))
+        block(joint_backward(half))
+        for item in chunks(reduce_plan, JOINT)[3 * half : 3 * half + 3]:
+            block(joint_gradient(*item))
+
+    @block
+    def first_norm_backward():
+        norm_backward(unit1, scale1, FIRST_GAIN, resid, False, (FIRST_GAIN, FIRST_SHIFT, EMBED_BIAS))
+
+    rows_embed = sizes[EMBED][0]
+
+    def embed_gradient(start, count):
+        def run():
+            value = tn(stem[...], low[:, start : start + count]).astype(NARROW)
+            local_grad[EMBED][:, :, 0:rows_embed, start : start + count] = value.reshape(4, 2, rows_embed, count)
+
+        return run
+
+    for item in chunks(reduce_plan, EMBED):
+        block(embed_gradient(*item))
+
+    @block
+    def start_vectors():
+        vec_copy(0).start()
+
+    @block
+    def stem_backward():
+        value = nt(low[...], full[EMBED][...].reshape(stem_width, width))
+        hidden[:, 0:stem_width] = value.astype(NARROW)
+        store_stem.start()
+
+    work_left = iter(blocks)
+    steps = (
+        lambda k: next(work_left)(),
+        start_z,
+        start_x,
+        gather_z(0),
+        gather_z(1),
+        gather_z(2),
+        gather_x,
+        gather_y,
+        gather_core,
+        gather_sent,
+        reduce_1,
+        reduce_2,
+        reduce_3,
+        reduce_4,
+        reduce_5,
+        reduce_6,
+        reduce_7,
+        vec_gather,
+        vec_step,
+    )
+    for code in ORDER:
+        steps[code // 32](code % 32)
+    vec_out[...] = vec_sum[len(vec_partners)]
+    for n in range(len(vec_partners)):
+        vec_copy(n).wait_send()
+    store_stem.wait()
+
+
+def fused(mesh):
+    def local(
+        stem_features,
+        lengths,
+        embed_weight,
+        embed_bias,
+        before_gain,
+        before_shift,
+        joint_weight,
+        query_bias,
+        value_bias,
+        output_weight,
+        output_bias,
+        middle_gain,
+        middle_shift,
+        expand_weight,
+        expand_bias,
+        shrink_weight,
+        shrink_bias,
+        cotangent,
+    ):
+        _, tokens, stem_width = stem_features.shape
+        width = embed_weight.shape[1]
+        mlp = expand_weight.shape[1]
+        shards = (embed_weight, joint_weight, output_weight, expand_weight, shrink_weight)
+        sizes = [item.shape for item in shards]
+        fsdp = lax.axis_index(AXIS)
+
+        nine = jnp.stack(
+            [
+                embed_bias,
+                before_gain,
+                before_shift,
+                query_bias,
+                value_bias,
+                output_bias,
+                middle_gain,
+                middle_shift,
+                shrink_bias,
+            ]
+        )
+        piece = nine.shape[1]
+        owner = jnp.arange(width) // piece
+        rows_nine = jnp.where(owner[None] == fsdp, jnp.tile(nine, (1, width // piece)), 0)
+        owner = jnp.arange(mlp) // expand_bias.shape[0]
+        rows_expand = jnp.where(owner == fsdp, jnp.tile(expand_bias, mlp // expand_bias.shape[0]), 0)
+        rows_expand = rows_expand.reshape(mlp // width, width)
+        used = 9 + mlp // width
+        vec_in = jnp.concatenate([rows_nine, rows_expand, jnp.zeros((VECTOR_ROWS - used, width), NARROW)])
+        vec_in = vec_in.astype(NARROW)
+
+        gather_plan = (
+            [(EMBED,) + item for item in column_chunks(width, 384)]
+            + [(JOINT,) + item for item in column_chunks(3 * width, width)]
+            + [(OUT, 0, width)]
+            + [(EXPAND,) + item for item in column_chunks(mlp, width)]
+            + [(SHRINK,) + item for item in column_chunks(width, 128)]
+        )
+        reduce_plan = (
+            [(SHRINK,) + item for item in column_chunks(width, 256)]
+            + [(EXPAND,) + item for item in column_chunks(mlp, width)]
+            + [(OUT, 0, width)]
+            + [(JOINT, part * width + at, 384) for at in (0, 384) for part in range(3)]
+            + [(EMBED,) + item for item in column_chunks(width, 256)]
+        )
+        steps, folds = len(gather_plan), len(reduce_plan)
+        vmem, dma = pltpu.VMEM, pltpu.SemaphoreType.DMA
+
+        def shares(make):
+            splits = [reduce_split(n, rows) for n, (rows, _) in enumerate(sizes)]
+            return [make(rows, cols, max(share, 16), share + both) for (rows, cols), (share, both) in zip(sizes, splits)]
+
+        def square(cols):
+            return vmem((tokens, cols), NARROW)
+
+        scratch = dict(
+            full=[vmem((4, 2) + item, NARROW) for item in sizes],
+            shrink_grad=vmem((4, 2) + sizes[SHRINK], NARROW),
+            core_shrink=vmem((4, 2, sizes[SHRINK][0] // 2, width), NARROW),
+            core_embed=vmem((4, 2, sizes[EMBED][0] // 2, width), NARROW),
+            from_y=shares(lambda rows, cols, share, mine: vmem((4, 2, share, cols), NARROW)),
+            from_x=shares(lambda rows, cols, share, mine: vmem((4, mine, cols), NARROW)),
+            from_z=shares(lambda rows, cols, share, mine: vmem((3, mine, cols), NARROW)),
+            part_out=shares(lambda rows, cols, share, mine: vmem((mine, cols), NARROW)),
+            part_in=shares(lambda rows, cols, share, mine: vmem((mine, cols), NARROW)),
+            final=shares(lambda rows, cols, share, mine: vmem((rows // 2, cols), WIDE)),
+            resid=vmem((tokens, width), WIDE),
+            work=vmem((tokens, width), WIDE),
+            bias=square(tokens),
+            unit1=square(width),
+            unit2=square(width),
+            normed=square(width),
+            normed_mid=square(width),
+            mixed=square(width),
+            cot=square(width),
+            low=square(width),
+            scale1=vmem((tokens, 1), WIDE),
+            scale2=vmem((tokens, 1), WIDE),
+            proj=square(3 * width),
+            mixed_t=vmem((width, tokens), NARROW),
+            lse=vmem((16, tokens), WIDE),
+            delta=vmem((16, tokens), WIDE),
+            pull=square(mlp),
+            hidden=square(mlp),
+            stem=square(stem_width),
+            vecs=vmem((VECTOR_ROWS, width), WIDE),
+            vec_all=vmem((4, 2, VECTOR_ROWS, width), NARROW),
+            vec_sum=vmem((6, VECTOR_ROWS, width), WIDE),
+            vec_from=vmem((5, VECTOR_ROWS, width), WIDE),
+            fold=vmem((24, width), WIDE),
+            fill=dma((steps,)),
+            g_send=dma((9, steps)),
+            g_recv=dma((9, steps)),
+            r_send=dma((6, folds)),
+            r_recv=dma((6, folds)),
+            r_done=dma((folds,)),
+            load=dma((2,)),
+            v_send=dma((7,)),
+            v_recv=dma((7,)),
+            free=pltpu.SemaphoreType.REGULAR,
+        )
+        names = list(scratch)
+
+        def body(*refs):
+            fused_kernel(tokens, width, stem_width, mlp, sizes, gather_plan, reduce_plan, names, *refs)
+
+        far = pl.BlockSpec(memory_space=pl.ANY)
+        near = pl.BlockSpec(memory_space=pltpu.VMEM)
+        outs = pl.pallas_call(
+            body,
+            out_shape=(
+                jax.ShapeDtypeStruct((tokens, width), NARROW),
+                jax.ShapeDtypeStruct((tokens, stem_width), NARROW),
+            )
+            + tuple(jax.ShapeDtypeStruct(item, WIDE) for item in sizes)
+            + (jax.ShapeDtypeStruct((VECTOR_ROWS, width), WIDE),),
+            in_specs=[near, pl.BlockSpec(memory_space=pltpu.SMEM)] + [far] * 7,
+            out_specs=(far,) * 7 + (near,),
+            scratch_shapes=list(scratch.values()),
+            compiler_params=pltpu.CompilerParams(
+                collective_id=0, has_side_effects=True, vmem_limit_bytes=64 * 2**20
+            ),
+        )(vec_in, lengths, stem_features[0], cotangent[0], *shards)
+        act, stem_grad, grads, vec_out = outs[0], outs[1], outs[2:7], outs[7]
+        mine = lax.dynamic_slice(vec_out, (0, fsdp * piece), (9, piece))
+        mine_expand = vec_out[9:used].reshape(mlp)
+        mine_expand = lax.dynamic_slice(mine_expand, (fsdp * expand_bias.shape[0],), expand_bias.shape)
+        return (
+            act[None],
+            stem_grad[None],
+            grads[EMBED],
+            mine[EMBED_BIAS],
+            mine[FIRST_GAIN],
+            mine[FIRST_SHIFT],
+            grads[JOINT],
+            mine[QUERY_BIAS],
+            mine[VALUE_BIAS],
+            grads[OUT],
+            mine[OUT_BIAS],
+            mine[SECOND_GAIN],
+            mine[SECOND_SHIFT],
+            grads[EXPAND],
+            mine_expand,
+            grads[SHRINK],
+            mine[SHRINK_BIAS],
+        )
+
+    return local
 
 
 def normalize(values):
@@ -38,7 +982,7 @@
     return jnp.sum(matrix.astype(jnp.float32), axis=0)
 
 
-def local(
+def general(
     stem_features,
     lengths,
     embed_weight,
@@ -77,23 +1021,7 @@
         shrink_weight,
         shrink_bias,
     )
-    gathered = (
-        lax.all_gather(shards[0], "fsdp", axis=0, tiled=True),
-        lax.all_gather(shards[1], "fsdp", axis=0, tiled=True),
-        lax.all_gather(shards[2], "fsdp", axis=0, tiled=True),
-        lax.all_gather(shards[3], "fsdp", axis=0, tiled=True),
-        lax.all_gather(shards[4], "fsdp", axis=0, tiled=True),
-        lax.all_gather(shards[5], "fsdp", axis=0, tiled=True),
-        lax.all_gather(shards[6], "fsdp", axis=0, tiled=True),
-        lax.all_gather(shards[7], "fsdp", axis=0, tiled=True),
-        lax.all_gather(shards[8], "fsdp", axis=0, tiled=True),
-        lax.all_gather(shards[9], "fsdp", axis=0, tiled=True),
-        lax.all_gather(shards[10], "fsdp", axis=0, tiled=True),
-        lax.all_gather(shards[11], "fsdp", axis=0, tiled=True),
-        lax.all_gather(shards[12], "fsdp", axis=0, tiled=True),
-        lax.all_gather(shards[13], "fsdp", axis=0, tiled=True),
-        lax.all_gather(shards[14], "fsdp", axis=0, tiled=True),
-    )
+    gathered = tuple(lax.all_gather(item, AXIS, axis=0, tiled=True) for item in shards)
     (
         embedding,
         embed_offset,
@@ -153,23 +1081,7 @@
         residual + jnp.dot(hidden, shrink, preferred_element_type=wide) + shrink_offset.astype(wide)
     )
     activations = output.astype(narrow).reshape(rows, row_len, width)
-    backward_set = (
-        lax.all_gather(shards[0], "fsdp", axis=0, tiled=True),
-        lax.all_gather(shards[1], "fsdp", axis=0, tiled=True),
-        lax.all_gather(shards[2], "fsdp", axis=0, tiled=True),
-        lax.all_gather(shards[3], "fsdp", axis=0, tiled=True),
-        lax.all_gather(shards[4], "fsdp", axis=0, tiled=True),
-        lax.all_gather(shards[5], "fsdp", axis=0, tiled=True),
-        lax.all_gather(shards[6], "fsdp", axis=0, tiled=True),
-        lax.all_gather(shards[7], "fsdp", axis=0, tiled=True),
-        lax.all_gather(shards[8], "fsdp", axis=0, tiled=True),
-        lax.all_gather(shards[9], "fsdp", axis=0, tiled=True),
-        lax.all_gather(shards[10], "fsdp", axis=0, tiled=True),
-        lax.all_gather(shards[11], "fsdp", axis=0, tiled=True),
-        lax.all_gather(shards[12], "fsdp", axis=0, tiled=True),
-        lax.all_gather(shards[13], "fsdp", axis=0, tiled=True),
-        lax.all_gather(shards[14], "fsdp", axis=0, tiled=True),
-    )
+    backward_set = gathered
     embedding = backward_set[0]
     first_gain = backward_set[2]
     joint = backward_set[4]
@@ -244,84 +1156,20 @@
         shrink_grad,
         shrink_offset_grad,
     )
-    owned = (
-        lax.psum_scatter(terms[0], "fsdp", scatter_dimension=0, tiled=True),
-        lax.psum_scatter(terms[1], "fsdp", scatter_dimension=0, tiled=True),
-        lax.psum_scatter(terms[2], "fsdp", scatter_dimension=0, tiled=True),
-        lax.psum_scatter(terms[3], "fsdp", scatter_dimension=0, tiled=True),
-        lax.psum_scatter(terms[4], "fsdp", scatter_dimension=0, tiled=True),
-        lax.psum_scatter(terms[5], "fsdp", scatter_dimension=0, tiled=True),
-        lax.psum_scatter(terms[6], "fsdp", scatter_dimension=0, tiled=True),
-        lax.psum_scatter(terms[7], "fsdp", scatter_dimension=0, tiled=True),
-        lax.psum_scatter(terms[8], "fsdp", scatter_dimension=0, tiled=True),
-        lax.psum_scatter(terms[9], "fsdp", scatter_dimension=0, tiled=True),
-        lax.psum_scatter(terms[10], "fsdp", scatter_dimension=0, tiled=True),
-        lax.psum_scatter(terms[11], "fsdp", scatter_dimension=0, tiled=True),
-        lax.psum_scatter(terms[12], "fsdp", scatter_dimension=0, tiled=True),
-        lax.psum_scatter(terms[13], "fsdp", scatter_dimension=0, tiled=True),
-        lax.psum_scatter(terms[14], "fsdp", scatter_dimension=0, tiled=True),
+    owned = tuple(lax.psum_scatter(item, AXIS, scatter_dimension=0, tiled=True) for item in terms)
+    summed = lax.psum(owned, "dp")
+    return (activations, stem_gradient) + tuple(summed)
+
+
+def solution(mesh):
+    rows, whole, vector = P(("dp", AXIS), None, None), P(AXIS, None), P(AXIS)
+    params = (whole, vector, vector, vector, whole, vector, vector, whole, vector)
+    params = params + (vector, vector, whole, vector, whole, vector)
+    plain = mesh.shape["dp"] != 4 or mesh.shape[AXIS] != 8
+    return jax.shard_map(
+        general if plain else fused(mesh),
+        mesh=mesh,
+        in_specs=(rows, P(("dp", AXIS), None)) + params + (rows,),
+        out_specs=(rows, rows) + params,
+        check_vma=False,
     )
-    summed = lax.psum(
-        (
-            owned[0],
-            owned[1],
-            owned[2],
-            owned[3],
-            owned[4],
-            owned[5],
-            owned[6],
-            owned[7],
-            owned[8],
-            owned[9],
-            owned[10],
-            owned[11],
-            owned[12],
-            owned[13],
-            owned[14],
-        ),
-        "dp",
-    )
-    return (activations, stem_gradient) + tuple(summed)
-
-
-def solution(mesh):
-    in_specs = (
-        P(("dp", "fsdp"), None, None),
-        P(("dp", "fsdp"), None),
-        P("fsdp", None),
-        P("fsdp"),
-        P("fsdp"),
-        P("fsdp"),
-        P("fsdp", None),
-        P("fsdp"),
-        P("fsdp"),
-        P("fsdp", None),
-        P("fsdp"),
-        P("fsdp"),
-        P("fsdp"),
-        P("fsdp", None),
-        P("fsdp"),
-        P("fsdp", None),
-        P("fsdp"),
-        P(("dp", "fsdp"), None, None),
-    )
-    out_specs = (
-        P(("dp", "fsdp"), None, None),
-        P(("dp", "fsdp"), None, None),
-        P("fsdp", None),
-        P("fsdp"),
-        P("fsdp"),
-        P("fsdp"),
-        P("fsdp", None),
-        P("fsdp"),
-        P("fsdp"),
-        P("fsdp", None),
-        P("fsdp"),
-        P("fsdp"),
-        P("fsdp"),
-        P("fsdp", None),
-        P("fsdp"),
-        P("fsdp", None),
-        P("fsdp"),
-    )
-    return jax.shard_map(local, mesh=mesh, in_specs=in_specs, out_specs=out_specs, check_vma=False)

time: 1070 us -> 197 us (0.18)
  waiting for transfers between devices: 727 us -> 0 us
  Pallas kernels: 0 us -> 179 us
  matrix products: 146 us -> 0 us
  blocking collectives: 108 us -> 0 us
  other arithmetic: 29.9 us -> 0.74 us
  local copies, waits for them, and re-layouts: 30.6 us -> 13.9 us
  between operations: 16.7 us -> 0.97 us
    reduce_scatter x5 -> x0, waiting for transfers between devices: 529 us -> none  [the longest x1 167 us: local(): lax.psum_scatter(terms[11], 'fsdp', scatter_dimension=0, tiled=True)]
    pallas_call x0 -> x1, Pallas kernels: none -> 179 us  [local(): pl.pallas_call(body, out_shape=(jax.ShapeDtypeStruct((tokens, width), NAR...]
    all_gather x5 -> x0, waiting for transfers between devices: 168 us -> none  [the longest x1 77.2 us: local(): lax.all_gather(shards[11], 'fsdp', axis=0, tiled=True)]
    dot_general x21 -> x0, matrix products: 146 us -> none  [the longest x1 22.2 us: local(): jnp.dot(normed_mid, expand, preferred_element_type=wide)]
    unnamed x2 -> x0, blocking collectives: 75.5 us -> none
    psum x1 -> x0, waiting for transfers between devices: 26.6 us -> none  [local(): lax.psum((owned[0], owned[1], owned[2], owned[3], owned[4], owned[5], own...]
    all_gather x1 -> x0, blocking collectives: 26 us -> none  [local(): lax.all_gather(shards[12], 'fsdp', axis=0, tiled=True)]
    convert_element_type x10 -> x0, other arithmetic: 15.1 us -> none  [the longest x1 12.7 us: local(): scores_grad = (attend_wide * (attend_grad - centered)).astype(narrow)]
  transfers between devices with their start and end apart: 11 -> 0, of which waited for: 9 -> 0; matrix products, arithmetic and copies ran while one was open for 16% -> 0% of each run, Pallas kernels for 0% -> 0%
where the time goes in v1:
time: 197 us; the launch traced here: 194 us
  Pallas kernels  179 us (91%)
  local copies, waits for them, and re-layouts  13.9 us (7%)
    pallas_call x1, Pallas kernels, local(): pl.pallas_call(body, out_shape=(jax.ShapeDtypeStruct((tokens, width), NAR...  179 us
    unnamed x19, local copies, waits for them, and re-layouts  8.46 us

profile of v1, /device:TPU:0, one launch (start us, length us, event | category | flops | bytes accessed | tf_op | source)
XLA Modules:
  0.0 194.1 jit_solution(15517649422044623486)
XLA Ops:
  0.7 1.5 stack.39
  2.2 0.1 tile.21
  2.3 0.7 tile.22
  3.0 0.1 pad.2.clone
  3.1 0.7 maximum_maximum_fusion.refs_0_
  3.8 178.5 %shard_map.305 = (bf16[576,768]{1,0:T(8,128)(2,1)}, bf16[576,1024]{1,0:T(8,128)(2,1)}, f32[128,768]{1,0:T(8,128)}, f32[96,2304]{1,0:T(8,128)}, f32[96,768]{1,0:T...) custom-call(bf16[16,768]{1,0:T(8,128)(2,1)} %maximum_maximum_fusion.refs_0_, s32[1,6]{1,0:T(1,128)} %refs_1_.1, ...), custom_call_target="tpu_custom_call" | custom-call | tf_op jit(solution)/shard_map/pallas_call | solution.py:914
  182.3 0.0 copy-start.2
  182.3 1.6 dynamic-slice_bitcast_fusion
  184.0 0.7 slice.38
  184.7 0.7 dynamic_slice.7
  185.4 2.1 %copy.42 = bf16[1,576,768]{2,1,0:T(8,128)(2,1)} copy(bf16[1,576,768]{2,1,0:T(8,128)(2,1)} %bitcast.34) | data formatting | bytes 1769472
  187.5 0.0 copy-done.2
  187.5 0.0 copy-start.4
  187.5 0.0 copy-start.3
  187.5 1.0 copy.43
  188.5 0.2 copy-done.4
  188.8 0.0 copy-start.5
  188.8 0.7 copy.44
  189.5 0.0 copy-done.3
  189.5 0.0 copy-start.1
  189.5 0.9 copy.45
  190.4 0.0 copy-done.5
  190.4 0.7 copy.46
  191.1 0.0 copy-done.1
  191.1 0.0 copy-start
  191.1 1.0 copy.47
  192.2 0.7 copy-done
  192.8 1.0 copy.48
  (7 shorter events, 0.1 us)
Async XLA Ops:
  182.3 5.2 %copy-start.2 = (bf16[576,1024]{1,0:T(8,128)(2,1)S(1)}, bf16[576,1024]{1,0:T(8,128)(2,1)}, u32[]{:S(2)}) copy-start(bf16[576,1024]{1,0:T(8,128)(2,1)} %get-tuple-element.26) | copy-start | bytes 3538948
  187.5 1.2 copy-start.4
  187.5 2.0 %copy-start.3 = (f32[96,2304]{1,0:T(8,128)S(1)}, f32[96,2304]{1,0:T(8,128)}, u32[]{:S(2)}) copy-start(f32[96,2304]{1,0:T(8,128)} %get-tuple-element.65) | copy-start | bytes 2654212
  188.8 1.7 copy-start.5
  189.5 1.6 copy-start.1
  191.1 1.7 copy-start
